TPU v7x, 32 devices: a whole 2x2x4 slice. The times are simulated.
32 devices in a mesh: seq: 4 (over z), chan: 8 (over y, x, core).
Axes of the slice: x: 2, y: 2, z: 4, core: 2. Of those that a mesh axis runs over, the one named last changes fastest.
Arguments:
- query_rows: bfloat16 [16384, 4096], P(('seq', 'chan')), may hold values from -6 to 6
- key_rows: bfloat16 [16384, 4096], P(('seq', 'chan')), may hold values from -6 to 6
- value_rows: bfloat16 [16384, 4096], P(('seq', 'chan')), may hold values from -6 to 6
- residue: float32 [4096, 16], P('chan'), may hold values from -1.5 to 1.5
- pole_rate: float32 [4096, 16], P('chan'), may hold values from 1 to 512
- skip_gain: float32 [4096], P('chan'), may hold values from -4 to 4
- out_weight: bfloat16 [4096, 4096], P('chan', 'seq'), may hold values from -0.09375 to 0.09375
Outputs:
- projected: bfloat16 [4, 4096, 4096], P(None, 'chan', 'seq')
All inputs are finite; a program needn't handle non-finite values.
Results may differ from a plain program's by a relative error of at most 0.014.
Values may be sent and summed in bfloat16 or wider, within the bound.
A program may use at most 512 MiB of HBM per device.

v0:
```python
import math

import jax
import jax.numpy as jnp
from jax import lax
from jax.sharding import PartitionSpec as P

SPANS = 16


precise = lax.Precision.HIGHEST
three_pass = lax.Precision.HIGH


def forward_matrix(block_len):
    frequency = jnp.arange(block_len, dtype=jnp.int32)
    position = jnp.arange(block_len, dtype=jnp.int32)
    phases = frequency[:, None] * position[None, :] % (2 * block_len)
    angles = phases.astype(jnp.float32) * (math.pi / block_len)
    real_rows = jnp.cos(angles)
    alternate = jnp.where(position % 2 == 0, 1.0, -1.0).astype(jnp.float32)
    imag_rows = jnp.where(frequency[:, None] == 0, alternate[None, :], -jnp.sin(angles))
    return jnp.concatenate([real_rows, imag_rows], axis=0)


def split_matrix(matrix):
    upper_part = matrix.astype(jnp.bfloat16)
    lower_part = (matrix - upper_part.astype(jnp.float32)).astype(jnp.bfloat16)
    return (upper_part, lower_part)


def inverse_matrix(block_len):
    outputs = jnp.arange(block_len, dtype=jnp.int32) + block_len
    frequency = jnp.arange(block_len, dtype=jnp.int32)
    phases = outputs[:, None] * frequency[None, :] % (2 * block_len)
    angles = phases.astype(jnp.float32) * (math.pi / block_len)
    scaling = jnp.where(frequency[None, :] == 0, 1.0, 2.0).astype(jnp.float32) / (2.0 * block_len)
    real_cols = scaling * jnp.cos(angles)
    alternate = (jnp.where(outputs % 2 == 0, 1.0, -1.0).astype(jnp.float32) / (2.0 * block_len))[
        :, None
    ]
    imag_cols = jnp.where(frequency[None, :] == 0, alternate, -scaling * jnp.sin(angles))
    return jnp.concatenate([real_cols, imag_cols], axis=1)


def pole_spectra(decay_rate, block_len):
    frequency = jnp.arange(block_len, dtype=jnp.int32)
    angles = (frequency.astype(jnp.float32) * (math.pi / block_len))[:, None, None]
    retain = jnp.exp(-decay_rate)[None]
    leakage = -jnp.expm1(-decay_rate)[None]
    real_den = 2.0 * jnp.square(jnp.sin(0.5 * angles)) + leakage * jnp.cos(angles)
    imag_den = retain * jnp.sin(angles)
    modulus = real_den * real_den + imag_den * imag_den
    real_part = real_den / modulus
    imag_part = jnp.where(frequency[:, None, None] == 0, 1.0 / (1.0 + retain), -imag_den / modulus)
    return jnp.concatenate([real_part, imag_part], axis=0)


def lag_spectra(pole_terms, plain_sum, weight, decay_rate, lag_steps, block_len):
    lag_float = lag_steps.astype(jnp.float32)[:, None, None]
    later = (
        weight[None]
        * jnp.exp(-decay_rate[None] * (block_len * jnp.maximum(lag_float - 1.0, 0.0)))
        * (-jnp.expm1(-2.0 * block_len * decay_rate))[None]
    )
    first = -weight * jnp.exp(-decay_rate * block_len)
    lag_weight = jnp.where(lag_float >= 1.0, later, jnp.where(lag_float == 0.0, first[None], 0.0))
    summed = jnp.einsum("kcm,rcm->krc", pole_terms, lag_weight, precision=precise)
    parity = jnp.where(jnp.arange(2 * block_len) % 2 == 0, 1.0, -1.0).astype(jnp.float32)
    at_zero = (lag_steps == 0).astype(jnp.float32)
    return summed + parity[:, None, None] * at_zero[None, :, None] * plain_sum[:, None, :]


def packed_product(left_side, right_side, block_len):
    column_shape = (block_len,) + (1,) * (left_side.ndim - 1)
    inner_mask = (jnp.arange(block_len) > 0).astype(jnp.float32).reshape(column_shape)
    left_real, left_imag = (left_side[:block_len], left_side[block_len:])
    right_real, right_imag = (right_side[:block_len], right_side[block_len:])
    real_out = left_real * right_real - inner_mask * left_imag * right_imag
    cross_term = left_real * right_imag + left_imag * right_real
    imag_out = inner_mask * cross_term + (1.0 - inner_mask) * left_imag * right_imag
    return jnp.concatenate([real_out, imag_out], axis=0)


def to_spectra(signal_bf, matrix_pair, block_len):
    seq_rows, channels = signal_bf.shape
    block_count = seq_rows // block_len
    arranged = (
        signal_bf.reshape(block_count, block_len, channels)
        .transpose(1, 0, 2)
        .reshape(block_len, block_count * channels)
    )
    spectrum = jnp.dot(matrix_pair[0], arranged, preferred_element_type=jnp.float32)
    spectrum = spectrum + jnp.dot(matrix_pair[1], arranged, preferred_element_type=jnp.float32)
    return spectrum.reshape(2 * block_len, block_count, channels)


def from_spectra(spectrum, matrix, block_len):
    block_count, channels = (spectrum.shape[1], spectrum.shape[2])
    flat = jnp.dot(
        matrix,
        spectrum.reshape(2 * block_len, block_count * channels),
        precision=three_pass,
        preferred_element_type=jnp.float32,
    )
    return (
        flat.reshape(block_len, block_count, channels)
        .transpose(1, 0, 2)
        .reshape(block_count * block_len, channels)
    )


def on_device(query_rows, key_rows, value_rows, residue, pole_rate, skip_gain, out_weight):
    product = (key_rows.astype(jnp.float32) * value_rows.astype(jnp.float32)).astype(jnp.bfloat16)
    received = lax.all_to_all(product, "chan", split_axis=1, concat_axis=0, tiled=True)
    seq_rows, channels = received.shape
    seq_count = lax.axis_size("seq")
    block_len = seq_rows * seq_count // SPANS
    own_count = seq_rows // block_len
    own_index = lax.axis_index("seq")
    own_first = own_index * own_count
    signal = received.astype(jnp.float32)
    decay_rate = pole_rate / (seq_rows * seq_count)
    weight = residue * jnp.sqrt(2.0 * decay_rate)
    pole_terms = pole_spectra(decay_rate, block_len)
    plain_sum = jnp.einsum("kcm,cm->kc", pole_terms, weight, precision=precise)
    forward = split_matrix(forward_matrix(block_len))
    inverse = inverse_matrix(block_len)
    zero_spectra = jnp.zeros((2 * block_len, own_count, channels), jnp.float32)
    piece_rows = lax.all_gather(received, "seq", axis=0, tiled=True)

    def make_spectrum():
        return to_spectra(piece_rows, forward, block_len)

    block_count = piece_rows.shape[0] // block_len

    def process(partial_value):
        spectrum = make_spectrum()
        lag_steps = (
            own_first - (block_count - 1) + jnp.arange(own_count + block_count - 1, dtype=jnp.int32)
        )
        lagged = lag_spectra(pole_terms, plain_sum, weight, decay_rate, lag_steps, block_len)

        def one_source(source_index, inner_sum):
            window = lax.dynamic_slice_in_dim(lagged, block_count - 1 - source_index, own_count, 1)
            source = lax.dynamic_index_in_dim(spectrum, source_index, 1, keepdims=True)
            return inner_sum + packed_product(window, source, block_len)

        return lax.fori_loop(0, block_count, one_source, partial_value)

    def unchanged(partial_value):
        return partial_value

    gathered = lax.cond(
        jnp.int32(0) // block_len < own_first + own_count, process, unchanged, zero_spectra
    )
    convolved = from_spectra(gathered, inverse, block_len)
    mixed = (convolved + skip_gain[None, :] * signal).astype(jnp.bfloat16)
    regrouped = lax.all_to_all(mixed, "chan", split_axis=0, concat_axis=1, tiled=True)
    gated = (query_rows.astype(jnp.float32) * regrouped.astype(jnp.float32)).astype(jnp.bfloat16)
    token_block = lax.all_gather(gated, "seq", axis=0, tiled=True)
    result = jnp.dot(
        token_block,
        lax.all_gather(out_weight, "chan", axis=0, tiled=True),
        preferred_element_type=jnp.float32,
    )
    return result.astype(jnp.bfloat16).reshape(seq_count, query_rows.shape[0], out_weight.shape[1])


def solution(mesh):
    in_specs = (
        P(("seq", "chan"), None),
        P(("seq", "chan"), None),
        P(("seq", "chan"), None),
        P("chan", None),
        P("chan", None),
        P("chan"),
        P("chan", "seq"),
    )
    out_specs = P(None, "chan", "seq")
    return jax.shard_map(
        on_device, mesh=mesh, in_specs=in_specs, out_specs=out_specs, check_vma=False
    )
```

profile of v0, /device:TPU:0, one launch (start us, length us, event | category | flops | bytes accessed | tf_op | source)
XLA Modules:
  0.0 2774.9 jit_solution(10353206575951625568)
XLA Ops:
  11.9 54.1 %all_to_all.29 = bf16[512,8,512]{2,0,1:T(8,128)(2,1)} all-to-all(bf16[512,8,512]{2,0,1:T(8,128)(2,1)S(1)} %bitcast.68), channel_id=1, replica_groups=mesh['seq'=4,'chan'=8] {'chan'}, dimensions={1} | all-to-all | bytes 8388608 | tf_op jit(solution)/shard_map/all_to_all | solution.py:115
  94.5 41.6 %fusion.53 = f32[512,1,2048]{2,1,0:T(1,128)} fusion(f32[512,16,1]{1,2,0:T(1,128)S(1)} %copy.44, f32[1024,512,16]{0,2,1:T(8,128)} %get-tuple-element.203, f32[1024,512,16]{0,2,1:T(8,128)} %get-tuple-element.202), kind=kOutput, calls=%fused_computation.115 | convolution fusion | flops 218103808 | bytes 71335936 | tf_op jit(solution)/shard_map/kcm,cm->kc/dot_general | solution.py:126
  157.8 34.4 %cosine_multiply_fusion = (f32[1024,1024]{1,0:T(8,128)}, f32[1024,1024]{1,0:T(8,128)}, f32[1024,1024]{1,0:T(8,128)S(1)}) fusion(s32[1024]{0:T(1024)S(1)} %iota_add_fusion.1, f32[1024]{0:T(1024)S(1)} %get-tuple-element.214, f32[1024]{0:T(1024)S(1)} %get-tuple-element.216, f32[1024]{0:T(1024)S(1)} %get-tuple-element.213, ...), kind=kLoop, calls=%fused_computation.81 | loop fusion | flops 34603008 | bytes 12604416 | tf_op jit(solution)/shard_map/mul | solution.py:38
  197.5 45.0 %pad_maximum_fusion = f32[2048,512,16]{0,2,1:T(8,128)} fusion(f32[1024,512,16]{0,2,1:T(8,128)} %get-tuple-element.203, f32[1024,512,16]{0,2,1:T(8,128)} %get-tuple-element.202), kind=kLoop, calls=%fused_computation.44 | loop fusion | flops 16777216 | bytes 134217728 | tf_op jit(solution)/shard_map/concatenate | solution.py:56
  242.4 110.0 %all-gather.4.cloned.1.call-done = bf16[16384,512]{1,0:T(8,128)(2,1)} async-done(((bf16[4096,512]{1,0:T(8,128)(2,1)}), bf16[16384,512]{1,0:T(8,128)(2,1)}) %all-gather.4.cloned.1.call-update) | async-done | bytes 16777232 | tf_op jit(solution)/shard_map/all_gather | solution.py:130
  352.4 1977.7 %conditional.1 = (f32[2048,4,512]{2,1,0:T(4,128)}) conditional(s32[]{:T(128)} %convert_element_type.122, () %tuple.33, (s32[]{:T(128)}, f32[512,16]{0,1:T(8,128)S(1)}, f32[512,16]{1,0:T(8,128)S(1)}, f32[2048,512,16]{0,2,1:T(8,128)}, f32[2048,512]{0,1:T(8,128)}, /*index=5*/bf16[16384,512]{1,0:T(8,128)(2,1)}, bf16[2048,1024]{1,0:T(8,128)(2,1)}, ...), branch_computations={%region_0.1_spmd, %region_1.4_spmd} | conditional | flops 72637849600 | bytes 793428672 | solution.py:154
  352.8 112.6 %bitcast_add_fusion = f32[2048,19,512]{0,1,2:T(8,128)} fusion(f32[2048,512]{0,1:T(8,128)} %get-tuple-element.137, f32[2048,19]{0,1:T(8,128)S(1)} %broadcast_multiply_fusion, f32[2048,512,16]{0,2,1:T(8,128)} %get-tuple-element.136, f32[512,16]{1,0:T(8,128)S(1)} %get-tuple-element.198, f32[512,16]{1,0:T(8,128)S(1)} %get-tuple-element.199, ...), kind=kOutput, calls=%fused_computation.12 | convolution fusion | flops 3865829376 | bytes 151281776 | tf_op jit(solution)/shard_map/cond/branch_1_fun/kcm,rcm->krc/dot_general | solution.py:68
  487.1 44.9 %fusion.55 = f32[2048,8192]{1,0:T(8,128)} fusion(bf16[2048,1024]{1,0:T(8,128)(2,1)} %get-tuple-element.138, bf16[1024,8192]{0,1:T(8,128)(2,1)} %bitcast.66), kind=kOutput, calls=%fused_computation.117 | convolution fusion | flops 34359738368 | bytes 88080384 | tf_op jit(solution)/shard_map/cond/branch_1_fun/dot_general | solution.py:93
  532.1 63.6 %convolution_add_fusion = f32[2048,8192]{1,0:T(8,128)} fusion(f32[2048,8192]{1,0:T(8,128)} %fusion.55, bf16[2048,1024]{1,0:T(8,128)(2,1)} %get-tuple-element.140, bf16[1024,8192]{0,1:T(8,128)(2,1)} %bitcast.67), kind=kOutput, calls=%fused_computation.13 | convolution fusion | flops 34376515584 | bytes 155189248 | tf_op jit(solution)/shard_map/cond/branch_1_fun/dot_general | solution.py:94
  595.7 70.1 %copy.52 = f32[256,8,16,512]{3,2,1,0:T(8,128)} copy(f32[256,8,16,512]{3,1,2,0:T(8,128)} %bitcast.22) | data formatting | bytes 134217728 | tf_op jit(solution)/shard_map/cond
  665.8 1664.2 %while.15 = (s32[]{:T(128)}, f32[2048,4,512]{2,1,0:T(4,128)}, f32[2048,19,512]{0,1,2:T(8,128)}, f32[2048,16,512]{2,1,0:T(8,128)}, s32[]{:T(128)}, /*index=5*/s32[]{:T(128)}, s32[]{:T(128)}, s32[]{:T(128)}, s32[]{}) while((s32[]{:T(128)}, f32[2048,4,512]{2,1,0:T(4,128)}, f32[2048,19,512]{0,1,2:T(8,128)}, ...), condition=%wide.region_3.3_spmd.clone, body=%wide.region_2.2_spmd.clone.sunk | while | flops 35656712 | bytes 230703376 | solution.py:149
  666.0 29.0 %constant_dynamic-slice_fusion.6 = (f32[1024,4,512]{0,1,2:T(4,128)}, f32[1024,4,512]{0,1,2:T(4,128)}) fusion(f32[2048,19,512]{0,1,2:T(8,128)} %get-tuple-element.278, s32[]{:T(128)S(6)} %select_n.185, s32[]{:T(128)S(6)} %add.280), kind=kLoop, calls=%fused_computation.9.clone.1 | loop fusion | bytes 33554440 | tf_op jit(solution)/shard_map/cond/branch_1_fun/while/body/eval_jaxpr/slice | solution.py:77
  871.8 29.0 %constant_dynamic-slice_fusion.6 = (f32[1024,4,512]{0,1,2:T(4,128)}, f32[1024,4,512]{0,1,2:T(4,128)}) fusion(f32[2048,19,512]{0,1,2:T(8,128)} %get-tuple-element.278, s32[]{:T(128)S(6)} %select_n.185, s32[]{:T(128)S(6)} %add.280), kind=kLoop, calls=%fused_computation.9.clone.1 | loop fusion | bytes 33554440 | tf_op jit(solution)/shard_map/cond/branch_1_fun/while/body/eval_jaxpr/slice | solution.py:77
  976.0 29.0 %constant_dynamic-slice_fusion.6 = (f32[1024,4,512]{0,1,2:T(4,128)}, f32[1024,4,512]{0,1,2:T(4,128)}) fusion(f32[2048,19,512]{0,1,2:T(8,128)} %get-tuple-element.278, s32[]{:T(128)S(6)} %select_n.185, s32[]{:T(128)S(6)} %add.280), kind=kLoop, calls=%fused_computation.9.clone.1 | loop fusion | bytes 33554440 | tf_op jit(solution)/shard_map/cond/branch_1_fun/while/body/eval_jaxpr/slice | solution.py:77
  1184.3 29.0 %constant_dynamic-slice_fusion.6 = (f32[1024,4,512]{0,1,2:T(4,128)}, f32[1024,4,512]{0,1,2:T(4,128)}) fusion(f32[2048,19,512]{0,1,2:T(8,128)} %get-tuple-element.278, s32[]{:T(128)S(6)} %select_n.185, s32[]{:T(128)S(6)} %add.280), kind=kLoop, calls=%fused_computation.9.clone.1 | loop fusion | bytes 33554440 | tf_op jit(solution)/shard_map/cond/branch_1_fun/while/body/eval_jaxpr/slice | solution.py:77
  1288.5 29.0 %constant_dynamic-slice_fusion.6 = (f32[1024,4,512]{0,1,2:T(4,128)}, f32[1024,4,512]{0,1,2:T(4,128)}) fusion(f32[2048,19,512]{0,1,2:T(8,128)} %get-tuple-element.278, s32[]{:T(128)S(6)} %select_n.185, s32[]{:T(128)S(6)} %add.280), kind=kLoop, calls=%fused_computation.9.clone.1 | loop fusion | bytes 33554440 | tf_op jit(solution)/shard_map/cond/branch_1_fun/while/body/eval_jaxpr/slice | solution.py:77
  1496.8 29.0 %constant_dynamic-slice_fusion.6 = (f32[1024,4,512]{0,1,2:T(4,128)}, f32[1024,4,512]{0,1,2:T(4,128)}) fusion(f32[2048,19,512]{0,1,2:T(8,128)} %get-tuple-element.278, s32[]{:T(128)S(6)} %select_n.185, s32[]{:T(128)S(6)} %add.280), kind=kLoop, calls=%fused_computation.9.clone.1 | loop fusion | bytes 33554440 | tf_op jit(solution)/shard_map/cond/branch_1_fun/while/body/eval_jaxpr/slice | solution.py:77
  1600.9 29.0 %constant_dynamic-slice_fusion.6 = (f32[1024,4,512]{0,1,2:T(4,128)}, f32[1024,4,512]{0,1,2:T(4,128)}) fusion(f32[2048,19,512]{0,1,2:T(8,128)} %get-tuple-element.278, s32[]{:T(128)S(6)} %select_n.185, s32[]{:T(128)S(6)} %add.280), kind=kLoop, calls=%fused_computation.9.clone.1 | loop fusion | bytes 33554440 | tf_op jit(solution)/shard_map/cond/branch_1_fun/while/body/eval_jaxpr/slice | solution.py:77
  1809.3 29.0 %constant_dynamic-slice_fusion.6 = (f32[1024,4,512]{0,1,2:T(4,128)}, f32[1024,4,512]{0,1,2:T(4,128)}) fusion(f32[2048,19,512]{0,1,2:T(8,128)} %get-tuple-element.278, s32[]{:T(128)S(6)} %select_n.185, s32[]{:T(128)S(6)} %add.280), kind=kLoop, calls=%fused_computation.9.clone.1 | loop fusion | bytes 33554440 | tf_op jit(solution)/shard_map/cond/branch_1_fun/while/body/eval_jaxpr/slice | solution.py:77
  1913.4 29.0 %constant_dynamic-slice_fusion.6 = (f32[1024,4,512]{0,1,2:T(4,128)}, f32[1024,4,512]{0,1,2:T(4,128)}) fusion(f32[2048,19,512]{0,1,2:T(8,128)} %get-tuple-element.278, s32[]{:T(128)S(6)} %select_n.185, s32[]{:T(128)S(6)} %add.280), kind=kLoop, calls=%fused_computation.9.clone.1 | loop fusion | bytes 33554440 | tf_op jit(solution)/shard_map/cond/branch_1_fun/while/body/eval_jaxpr/slice | solution.py:77
  2017.6 29.0 %constant_dynamic-slice_fusion.6 = (f32[1024,4,512]{0,1,2:T(4,128)}, f32[1024,4,512]{0,1,2:T(4,128)}) fusion(f32[2048,19,512]{0,1,2:T(8,128)} %get-tuple-element.278, s32[]{:T(128)S(6)} %select_n.185, s32[]{:T(128)S(6)} %add.280), kind=kLoop, calls=%fused_computation.9.clone.1 | loop fusion | bytes 33554440 | tf_op jit(solution)/shard_map/cond/branch_1_fun/while/body/eval_jaxpr/slice | solution.py:77
  2363.4 33.3 %fusion.25 = f32[1024,4,512]{2,0,1:T(8,128)} fusion(f32[4,512,2048]{2,1,0:T(8,128)} %bitcast.65, f32[1024,1024]{1,0:T(8,128)} %get-tuple-element.209, f32[1024,1024]{1,0:T(8,128)} %get-tuple-element.208), kind=kOutput, calls=%fused_computation.53 | convolution fusion | flops 25771900928 | bytes 33554432 | tf_op jit(solution)/shard_map/dot_general | solution.py:100
  2401.6 52.8 %all_to_all.30 = bf16[8,512,512]{2,1,0:T(8,128)(2,1)S(1)} all-to-all(bf16[8,512,512]{2,1,0:T(8,128)(2,1)S(1)} %add_convert_fusion), channel_id=1, replica_groups=mesh['seq'=4,'chan'=8] {'chan'}, dimensions={0} | all-to-all | bytes 8388608 | tf_op jit(solution)/shard_map/all_to_all | solution.py:159
  2461.2 283.3 %all-gather.6.cloned.1.call-done = bf16[2048,4096]{1,0:T(8,128)(2,1)} async-done(((bf16[512,4096]{1,0:T(8,128)(2,1)}), bf16[2048,4096]{1,0:T(8,128)(2,1)}) %all-gather.6.cloned.1.call-update) | async-done | bytes 16777232 | tf_op jit(solution)/shard_map/all_gather | solution.py:161
  (296 shorter events, 1524.5 us)
Async XLA Ops:
  6.5 345.9 %all-gather.4.cloned.1.call-start = ((), (), s32[]{:S(2)}) async-start(), calls=%async_computation.2 | async-start | bytes 20971520 | tf_op jit(solution)/shard_map/all_gather | solution.py:130
  11.9 55.1 %copy-start.3 = (f32[512,16]{0,1:T(8,128)S(1)}, f32[512,16]{0,1:T(8,128)}, u32[]{:S(2)}) copy-start(f32[512,16]{0,1:T(8,128)} %param.15) | copy-start | bytes 98308
  11.9 55.4 %copy-start.4 = (f32[512,16]{0,1:T(8,128)S(1)}, f32[512,16]{0,1:T(8,128)}, u32[]{:S(2)}) copy-start(f32[512,16]{0,1:T(8,128)} %param.14) | copy-start | bytes 98308
  66.1 2395.1 %all-gather.8.cloned.1.call-start = ((), (), s32[]{:S(2)}) async-start(), calls=%async_computation.4 | async-start | bytes 9437184 | tf_op jit(solution)/shard_map/all_gather | solution.py:164
  66.8 2677.7 %all-gather.6.cloned.1.call-start = ((), (), s32[]{:S(2)}) async-start(), calls=%async_computation.3 | async-start | bytes 20971520 | tf_op jit(solution)/shard_map/all_gather | solution.py:161
  719.3 13.3 slice-start
  719.3 14.3 copy-start
  821.0 14.3 copy-start
  925.1 14.3 copy-start
  1029.3 14.3 copy-start
  1133.5 14.3 copy-start
  1237.6 14.3 copy-start
  1341.8 14.3 copy-start
  1445.9 14.3 copy-start
  1550.1 14.3 copy-start
  1654.3 14.3 copy-start
  1758.4 14.3 copy-start
  1862.6 14.3 copy-start
  1966.7 14.3 copy-start
  2070.9 14.3 copy-start
  2175.1 14.3 copy-start
  2279.2 14.3 copy-start
  2363.4 33.4 %copy-start.1 = (bf16[512,8,512]{2,0,1:T(8,128)(2,1)S(1)}, bf16[512,8,512]{2,0,1:T(8,128)(2,1)}, u32[]{:S(2)}) copy-start(bf16[512,8,512]{2,0,1:T(8,128)(2,1)} %all_to_all.29) | copy-start | bytes 12582916
  2363.4 33.4 %copy-start.5 = (f32[512]{0:T(512)S(1)}, f32[512]{0:T(512)}, u32[]{:S(2)}) copy-start(f32[512]{0:T(512)} %param.16) | copy-start | bytes 6148
  (32 other events, 248.3 us)
Sparse Core Ops, SparseCore 0:
  66.2 286.1 all-gather.3
  354.3 52.5 all-gather.7
  2461.3 283.1 all-gather.5
where the time goes:
time: 2790 us; the launch traced here: 2770 us
  local copies, waits for them, and re-layouts  1240 us (44%)
  other arithmetic  702 us (25%)
  waiting for transfers between devices  394 us (14%)
  matrix products  320 us (11%)
  blocking collectives  107 us (4%)
    slice x16, local copies, waits for them, and re-layouts, packed_product(): left_real, left_imag = (left_side[:block_len], left_side[block_len:])  464 us
    while x128, local copies, waits for them, and re-layouts  428 us
    add x16, other arithmetic, one_source(): return inner_sum + packed_product(window, source, block_len)  397 us
    all_gather x1, waiting for transfers between devices, on_device(): token_block = lax.all_gather(gated, 'seq', axis=0, tiled=True)  283 us
    slice x16, local copies, waits for them, and re-layouts, packed_product(): right_real, right_imag = (right_side[:block_len], right_side[block_len:])  204 us
    sub x16, other arithmetic, packed_product(): real_out = left_real * right_real - inner_mask * left_imag * right_imag  163 us
    dot_general x1, matrix products, lag_spectra(): jnp.einsum('kcm,rcm->krc', pole_terms, lag_weight, precision=precise)  113 us
    all_gather x1, waiting for transfers between devices, on_device(): piece_rows = lax.all_gather(received, 'seq', axis=0, tiled=True)  110 us
  transfers between devices with their start and end apart: 3, of which 2 were waited for; matrix products, arithmetic and copies ran while one was open for 79% of the time, Pallas kernels for 0%

commit v1 on v0

v1 whole, which is shorter than its diff:
```python
import functools

import jax
import jax.numpy as jnp
from jax import lax
from jax.experimental import pallas as pl
from jax.experimental.pallas import tpu as pltpu
from jax.sharding import PartitionSpec as P

LANES = 128
SEGS = 8
PIECES = 4


def block_width(channels):
    return 512 if channels % 512 == 0 else LANES


def tree_sum(terms):
    while len(terms) > 1:
        paired = [terms[i] + terms[i + 1] for i in range(0, len(terms) - 1, 2)]
        if len(terms) % 2:
            paired.append(terms[-1])
        terms = paired
    return terms[0]


def pole_rows(params_ref, lanes, order, length):
    rates = params_ref[order : 2 * order, lanes] / length
    weights = params_ref[0:order, lanes] * jnp.sqrt(2.0 * rates)
    return rates, weights


def spread(row):
    return jnp.broadcast_to(row, (SEGS, LANES))


def load_signal(key_ref, value_ref, lanes, signal_ref):
    product = key_ref[:, lanes].astype(jnp.float32) * value_ref[:, lanes].astype(jnp.float32)
    signal_ref[...] = product.astype(jnp.bfloat16).astype(jnp.float32)


def state_kernel(order, length, params_ref, key_ref, value_ref, ends_ref, final_ref, signal_ref):
    tokens = key_ref.shape[0]
    steps = tokens // SEGS
    behind = (SEGS - 1 - lax.broadcasted_iota(jnp.int32, (SEGS, LANES), 0)).astype(jnp.float32)
    for first in range(0, key_ref.shape[1], LANES):
        lanes = slice(first, first + LANES)
        load_signal(key_ref, value_ref, lanes, signal_ref)
        rates, _ = pole_rows(params_ref, lanes, order, length)
        retain = jnp.exp(-rates)
        factors = [spread(retain[m : m + 1]) for m in range(order)]

        def step(i, states):
            x = signal_ref[pl.ds(i, SEGS, stride=steps), :]
            return tuple(f * s + x for f, s in zip(factors, states))

        zero = jnp.zeros((SEGS, LANES), jnp.float32)
        states = lax.fori_loop(0, steps, step, (zero,) * order, unroll=4)
        for m in range(order):
            ends_ref[m * SEGS : (m + 1) * SEGS, lanes] = states[m]
            carried = states[m] * jnp.exp(-(steps * behind) * spread(rates[m : m + 1]))
            final_ref[m : m + 1, lanes] = jnp.sum(carried, axis=0, keepdims=True)


def output_kernel(
    order,
    length,
    params_ref,
    key_ref,
    value_ref,
    query_ref,
    ends_ref,
    initial_ref,
    gated_ref,
    signal_ref,
    mixed_ref,
):
    tokens = key_ref.shape[0]
    steps = tokens // SEGS
    place = lax.broadcasted_iota(jnp.int32, (SEGS, LANES), 0)
    for first in range(0, key_ref.shape[1], LANES):
        lanes = slice(first, first + LANES)
        load_signal(key_ref, value_ref, lanes, signal_ref)
        rates, weights = pole_rows(params_ref, lanes, order, length)
        retain = jnp.exp(-rates)
        factors = [spread(retain[m : m + 1]) for m in range(order)]
        gains = [spread(weights[m : m + 1]) for m in range(order)]
        direct = spread(params_ref[2 * order : 2 * order + 1, lanes])
        starts = []
        for m in range(order):
            ends = ends_ref[m * SEGS : (m + 1) * SEGS, lanes]
            before = spread(initial_ref[m : m + 1, lanes])
            entry = jnp.where(place == 0, before, pltpu.roll(ends, 1, 0))
            distance = 1
            while distance < SEGS:
                fade = jnp.exp(-float(steps * distance) * spread(rates[m : m + 1]))
                moved = jnp.where(place >= distance, pltpu.roll(entry, distance, 0), 0.0)
                entry = entry + fade * moved
                distance *= 2
            starts.append(entry)

        def step(i, states):
            x = signal_ref[pl.ds(i, SEGS, stride=steps), :]
            states = tuple(f * s + x for f, s in zip(factors, states))
            terms = [g * s for g, s in zip(gains, states)]
            mixed_ref[pl.ds(i, SEGS, stride=steps), :] = tree_sum(terms) + direct * x
            return states

        lax.fori_loop(0, steps, step, tuple(starts), unroll=4)
        mixed = mixed_ref[...].astype(jnp.bfloat16).astype(jnp.float32)
        gated = query_ref[:, lanes].astype(jnp.float32) * mixed
        gated_ref[:, lanes] = gated.astype(jnp.bfloat16)


def copies_to_all(block, axis, count):
    copies = jnp.broadcast_to(block[None], (count,) + block.shape)
    return lax.all_to_all(copies, axis, split_axis=0, concat_axis=0, tiled=True)


def on_device(query_rows, key_rows, value_rows, residue, pole_rate, skip_gain, out_weight):
    tokens, channels = query_rows.shape
    own_channels, order = residue.shape
    seq_count = lax.axis_size("seq")
    chan_count = lax.axis_size("chan")
    length = float(tokens * chan_count * seq_count)

    weight_rows = lax.all_gather(out_weight, "chan", axis=0, tiled=True)

    own_params = jnp.concatenate(
        [residue.T, pole_rate.T, skip_gain[None], jnp.zeros((7, own_channels), jnp.float32)], axis=0
    )
    param_rows = own_params.shape[0]
    params = copies_to_all(own_params, "chan", chan_count)
    params = params.transpose(1, 0, 2).reshape(param_rows, channels)

    width = block_width(channels // PIECES)
    limit = pltpu.CompilerParams(vmem_limit_bytes=40 * 1024 * 1024)
    signal_scratch = pltpu.VMEM((tokens, LANES), jnp.float32)

    def columns(rows, base=0):
        return pl.BlockSpec((rows, width), lambda j: (0, base + j))

    ends, final = pl.pallas_call(
        functools.partial(state_kernel, order, length),
        grid=(channels // width,),
        in_specs=[columns(param_rows), columns(tokens), columns(tokens)],
        out_specs=[columns(order * SEGS), columns(order)],
        out_shape=[
            jax.ShapeDtypeStruct((order * SEGS, channels), jnp.float32),
            jax.ShapeDtypeStruct((order, channels), jnp.float32),
        ],
        scratch_shapes=[signal_scratch],
        compiler_params=limit,
        cost_estimate=pl.CostEstimate(
            flops=2 * order * tokens * channels,
            bytes_accessed=4 * tokens * channels,
            transcendentals=0,
        ),
    )(params, key_rows, value_rows)

    finals = lax.all_to_all(final, "chan", split_axis=1, concat_axis=0, tiled=True)
    finals = finals.reshape(chan_count, order, own_channels)
    rates = pole_rate.T / length
    block_fade = jnp.exp(-rates * tokens)
    total = jnp.zeros((order, own_channels), jnp.float32)
    for j in range(chan_count):
        total = total * block_fade + finals[j]
    totals = copies_to_all(total, "seq", seq_count)
    range_fade = jnp.exp(-rates * (tokens * chan_count))
    own_range = lax.axis_index("seq")
    state = jnp.zeros((order, own_channels), jnp.float32)
    for s in range(seq_count - 1):
        state = jnp.where(s < own_range, state * range_fade + totals[s], state)
    entries = []
    for j in range(chan_count):
        entries.append(state)
        state = state * block_fade + finals[j]
    initial = lax.all_to_all(
        jnp.concatenate(entries, axis=0), "chan", split_axis=0, concat_axis=1, tiled=True
    )
    initial, weight_rows = lax.optimization_barrier((initial, weight_rows))

    piece = channels // PIECES
    result = jnp.zeros((seq_count * tokens, out_weight.shape[1]), jnp.float32)
    for p in range(PIECES):
        base = p * piece // width
        spec = functools.partial(columns, base=base)
        gated = pl.pallas_call(
            functools.partial(output_kernel, order, length),
            grid=(piece // width,),
            in_specs=[
                spec(param_rows),
                spec(tokens),
                spec(tokens),
                spec(tokens),
                spec(order * SEGS),
                spec(order),
            ],
            out_specs=columns(tokens),
            out_shape=jax.ShapeDtypeStruct((tokens, piece), jnp.bfloat16),
            scratch_shapes=[signal_scratch, signal_scratch],
            compiler_params=limit,
            cost_estimate=pl.CostEstimate(
                flops=4 * order * tokens * piece,
                bytes_accessed=8 * tokens * piece,
                transcendentals=0,
            ),
        )(params, key_rows, value_rows, query_rows, ends, initial)
        token_block = lax.all_gather(gated, "seq", axis=0, tiled=True)
        result = result + jnp.dot(
            token_block,
            weight_rows[p * piece : (p + 1) * piece],
            preferred_element_type=jnp.float32,
        )
    return result.astype(jnp.bfloat16).reshape(seq_count, tokens, out_weight.shape[1])


def solution(mesh):
    in_specs = (
        P(("seq", "chan"), None),
        P(("seq", "chan"), None),
        P(("seq", "chan"), None),
        P("chan", None),
        P("chan", None),
        P("chan"),
        P("chan", "seq"),
    )
    out_specs = P(None, "chan", "seq")
    return jax.shard_map(
        on_device, mesh=mesh, in_specs=in_specs, out_specs=out_specs, check_vma=False
    )
```

time: 2790 us -> 442 us (0.16)
  local copies, waits for them, and re-layouts: 1240 us -> 26.9 us
  other arithmetic: 702 us -> 1.06 us
  matrix products: 320 us -> 49.6 us
  waiting for transfers between devices: 394 us -> 251 us
  blocking collectives: 107 us -> 39.3 us
  Pallas kernels: 0 us -> 54.3 us
    slice x32 -> x0, local copies, waits for them, and re-layouts: 668 us -> none  [the longest x16 464 us: packed_product(): left_real, left_imag = (left_side[:block_len], left_side[block_len:])]
    while x128 -> x0, local copies, waits for them, and re-layouts: 428 us -> none
    add x17 -> x1, other arithmetic: 397 us -> 0.03 us  [on_device(): total = total * block_fade + finals[j]]
    dot_general x6 -> x4, matrix products: 320 us -> 49.6 us  [on_device(): jnp.dot(token_block, weight_rows[p * piece:(p + 1) * piece], preferred_el...]
    sub x32 -> x0, other arithmetic: 163 us -> none  [the longest x16 163 us: packed_product(): real_out = left_real * right_real - inner_mask * left_imag * right_imag]
    all_gather x2 -> x1, waiting for transfers between devices: 110 us -> 0.02 us  [on_device(): weight_rows = lax.all_gather(out_weight, 'chan', axis=0, tiled=True)]
    cond x1 -> x0, local copies, waits for them, and re-layouts: 70.1 us -> none
    all_to_all x2 -> x3, blocking collectives: 107 us -> 39.3 us  [the longest x1 17.5 us: copies_to_all(): return lax.all_to_all(copies, axis, split_axis=0, concat_axis=0, tiled=True)]
  transfers between devices with their start and end apart: 3 -> 6, of which waited for: 2 -> 5; matrix products, arithmetic and copies ran while one was open for 79% -> 8% of each run, Pallas kernels for 0% -> 10%
where the time goes in v1:
time: 442 us; the launch traced here: 441 us
  waiting for transfers between devices  251 us (57%)
  Pallas kernels  54.3 us (12%)
  matrix products  49.6 us (11%)
  blocking collectives  39.3 us (9%)
  local copies, waits for them, and re-layouts  26.9 us (6%)
  between operations  13.4 us (3%)
  starting transfers between devices  5.27 us (1%)
    all_gather x4, waiting for transfers between devices, on_device(): token_block = lax.all_gather(gated, 'seq', axis=0, tiled=True)  244 us
    dot_general x4, matrix products, on_device(): jnp.dot(token_block, weight_rows[p * piece:(p + 1) * piece], preferred_el...  49.6 us
    pallas_call x4, Pallas kernels, on_device(): pl.pallas_call(functools.partial(output_kernel, order, length), grid=(pie...  36.1 us
    unnamed x30, local copies, waits for them, and re-layouts  26 us
    pallas_call x1, Pallas kernels, on_device(): pl.pallas_call(functools.partial(state_kernel, order, length), grid=(chan...  18.2 us
    all_to_all x1, blocking collectives, copies_to_all(): return lax.all_to_all(copies, axis, split_axis=0, concat_axis=0, tiled=True)  17.5 us
    all_to_all x1, blocking collectives, on_device(): lax.all_to_all(final, 'chan', split_axis=1, concat_axis=0, tiled=True)  12.5 us
    all_to_all x1, blocking collectives, on_device(): lax.all_to_all(jnp.concatenate(entries, axis=0), 'chan', split_axis=0, co...  9.35 us
  transfers between devices with their start and end apart: 6, of which 5 were waited for; matrix products, arithmetic and copies ran while one was open for 8% of the time, Pallas kernels for 10%

profile of v1, /device:TPU:0, one launch (start us, length us, event | category | flops | bytes accessed | tf_op | source)
XLA Modules:
  0.0 440.8 jit_solution(12985853986613201367)
XLA Ops:
  8.3 17.5 %all_to_all.45 = f32[8,40,512]{2,1,0:T(8,128)S(1)} all-to-all(f32[8,40,512]{2,1,0:T(8,128)S(1)} %broadcast_in_dim.20), channel_id=1, replica_groups=mesh['seq'=4,'chan'=8] {'chan'}, dimensions={0} | all-to-all | bytes 1310720 | tf_op jit(solution)/shard_map/all_to_all | solution.py:118
  28.0 2.2 copy-done.5
  30.2 18.2 %shard_map.73 = (f32[128,4096]{1,0:T(8,128)S(1)}, f32[16,4096]{1,0:T(8,128)S(1)}) custom-call(f32[40,4096]{1,0:T(8,128)S(1)} %bitcast.136, bf16[512,4096]{1,0:T(8,128)(2,1)S(1)} %copy-done, bf16[512,4096]{1,0:T(8,128)(2,1)S(1)} %copy-done.5), custom_call_target="tpu_custom_call" | custom-call | flops 67108864 | bytes 8388608 | tf_op jit(solution)/shard_map/pallas_call | solution.py:144
  48.5 12.5 %all_to_all.46 = f32[16,8,512]{2,0,1:T(8,128)S(1)} all-to-all(f32[16,8,512]{2,0,1:T(8,128)S(1)} %bitcast.156), channel_id=1, replica_groups=mesh['seq'=4,'chan'=8] {'chan'}, dimensions={1} | all-to-all | bytes 524288 | tf_op jit(solution)/shard_map/all_to_all | solution.py:162
  61.7 5.1 %all-to-all-start.2 = ((f32[4,16,512]{2,1,0:T(8,128)}), f32[4,16,512]{2,1,0:T(8,128)S(1)}, u32[]{:S(2)}, u32[]{:S(2)}) async-start(f32[4,16,512]{2,1,0:T(8,128)} %broadcast_in_dim.21), calls=%async_computation.2 | async-start | bytes 262144 | tf_op jit(solution)/shard_map/all_to_all | solution.py:118
  66.8 5.9 %all-to-all-done.2 = f32[4,16,512]{2,1,0:T(8,128)S(1)} async-done(((f32[4,16,512]{2,1,0:T(8,128)}), f32[4,16,512]{2,1,0:T(8,128)S(1)}, u32[]{:S(2)}, u32[]{:S(2)}) %all-to-all-start.2) | async-done | bytes 131104 | tf_op jit(solution)/shard_map/all_to_all | solution.py:118
  72.9 9.3 %all_to_all.47 = f32[8,16,512]{2,1,0:T(8,128)S(1)} all-to-all(f32[8,16,512]{2,1,0:T(8,128)S(1)} %bitcast.158), channel_id=1, replica_groups=mesh['seq'=4,'chan'=8] {'chan'}, dimensions={0} | all-to-all | bytes 524288 | tf_op jit(solution)/shard_map/all_to_all | solution.py:179
  84.5 2.2 copy-done.6
  86.7 9.0 %shard_map.75 = bf16[512,1024]{1,0:T(8,128)(2,1)S(1)} custom-call(f32[40,4096]{1,0:T(8,128)S(1)} %bitcast.137, bf16[512,4096]{1,0:T(8,128)(2,1)S(1)} %copy-done.1, bf16[512,4096]{1,0:T(8,128)(2,1)S(1)} %copy-done.6, bf16[512,4096]{1,0:T(8,128)(2,1)} %query_ref.7, f32[128,4096]{1,0:T(8,128)S(1)} %get-tuple-element.9.ends_ref, f32[16,4096]{1,0:T(8,128)S(1)} %bitcast.141), custom_call_target="tpu_custom_call" | custom-call | flops 33554432 | bytes 4194304 | tf_op jit(solution)/shard_map/pallas_call | solution.py:189
  98.9 2.4 copy-done.7
  101.3 9.0 %shard_map.74 = bf16[512,1024]{1,0:T(8,128)(2,1)S(1)} custom-call(f32[40,4096]{1,0:T(8,128)S(1)} %bitcast.138, bf16[512,4096]{1,0:T(8,128)(2,1)S(1)} %copy-done.2, bf16[512,4096]{1,0:T(8,128)(2,1)S(1)} %copy-done.7, bf16[512,4096]{1,0:T(8,128)(2,1)} %query_ref.7, f32[128,4096]{1,0:T(8,128)S(1)} %get-tuple-element.9.ends_ref, f32[16,4096]{1,0:T(8,128)S(1)} %bitcast.142), custom_call_target="tpu_custom_call" | custom-call | flops 33554432 | bytes 4194304 | tf_op jit(solution)/shard_map/pallas_call | solution.py:189
  113.6 2.2 copy-done.8
  115.8 9.0 %shard_map.76 = bf16[512,1024]{1,0:T(8,128)(2,1)S(1)} custom-call(f32[40,4096]{1,0:T(8,128)S(1)} %bitcast.139, bf16[512,4096]{1,0:T(8,128)(2,1)S(1)} %copy-done.3, bf16[512,4096]{1,0:T(8,128)(2,1)S(1)} %copy-done.8, bf16[512,4096]{1,0:T(8,128)(2,1)} %query_ref.7, f32[128,4096]{1,0:T(8,128)S(1)} %get-tuple-element.9.ends_ref, f32[16,4096]{1,0:T(8,128)S(1)} %bitcast.143), custom_call_target="tpu_custom_call" | custom-call | flops 33554432 | bytes 4194304 | tf_op jit(solution)/shard_map/pallas_call | solution.py:189
  125.9 2.2 copy-done.4
  128.1 2.2 copy-done.9
  130.3 9.1 %shard_map.77 = bf16[512,1024]{1,0:T(8,128)(2,1)S(1)} custom-call(f32[40,4096]{1,0:T(8,128)S(1)} %bitcast.140, bf16[512,4096]{1,0:T(8,128)(2,1)S(1)} %copy-done.4, bf16[512,4096]{1,0:T(8,128)(2,1)S(1)} %copy-done.9, bf16[512,4096]{1,0:T(8,128)(2,1)} %query_ref.7, f32[128,4096]{1,0:T(8,128)S(1)} %get-tuple-element.9.ends_ref, f32[16,4096]{1,0:T(8,128)S(1)} %bitcast.144), custom_call_target="tpu_custom_call" | custom-call | flops 33554432 | bytes 4194304 | tf_op jit(solution)/shard_map/pallas_call | solution.py:189
  140.4 34.3 %all-gather.10.cloned.1.call-done = bf16[2048,1024]{1,0:T(8,128)(2,1)} async-done(((bf16[512,1024]{1,0:T(8,128)(2,1)}), bf16[2048,1024]{1,0:T(8,128)(2,1)}) %all-gather.10.cloned.1.call-update) | async-done | bytes 4194320 | tf_op jit(solution)/shard_map/all_gather | solution.py:210
  174.7 10.8 %fusion.3 = f32[2048,1024]{1,0:T(8,128)} fusion(bf16[2048,1024]{1,0:T(8,128)(2,1)} %all-gather.10.cloned.1.call-done, bf16[4096,1024]{1,0:T(8,128)(2,1)} %all-gather.6.cloned.1.call-done), kind=kOutput, calls=%fused_computation.4 | convolution fusion | flops 4294967296 | bytes 14680064 | tf_op jit(solution)/shard_map/dot_general | solution.py:211
  185.5 70.1 %all-gather.8.cloned.1.call-done = bf16[2048,1024]{1,0:T(8,128)(2,1)} async-done(((bf16[512,1024]{1,0:T(8,128)(2,1)}), bf16[2048,1024]{1,0:T(8,128)(2,1)}) %all-gather.8.cloned.1.call-update) | async-done | bytes 4194320 | tf_op jit(solution)/shard_map/all_gather | solution.py:210
  255.7 10.7 %fusion.5 = f32[2048,1024]{1,0:T(8,128)} fusion(bf16[2048,1024]{1,0:T(8,128)(2,1)} %all-gather.8.cloned.1.call-done, bf16[4096,1024]{1,0:T(8,128)(2,1)} %all-gather.6.cloned.1.call-done), kind=kOutput, calls=%fused_computation.6 | convolution fusion | flops 4294967296 | bytes 14680064 | tf_op jit(solution)/shard_map/dot_general | solution.py:211
  266.4 70.0 %all-gather.12.cloned.1.call-done = bf16[2048,1024]{1,0:T(8,128)(2,1)} async-done(((bf16[512,1024]{1,0:T(8,128)(2,1)}), bf16[2048,1024]{1,0:T(8,128)(2,1)}) %all-gather.12.cloned.1.call-update) | async-done | bytes 4194320 | tf_op jit(solution)/shard_map/all_gather | solution.py:210
  336.4 10.9 %fusion.1 = f32[2048,1024]{1,0:T(8,128)} fusion(bf16[2048,1024]{1,0:T(8,128)(2,1)} %all-gather.12.cloned.1.call-done, bf16[4096,1024]{1,0:T(8,128)(2,1)} %all-gather.6.cloned.1.call-done), kind=kOutput, calls=%fused_computation.2 | convolution fusion | flops 4294967296 | bytes 14680064 | tf_op jit(solution)/shard_map/dot_general | solution.py:211
  347.3 69.8 %all-gather.14.cloned.1.call-done = bf16[2048,1024]{1,0:T(8,128)(2,1)} async-done(((bf16[512,1024]{1,0:T(8,128)(2,1)}), bf16[2048,1024]{1,0:T(8,128)(2,1)}) %all-gather.14.cloned.1.call-update) | async-done | bytes 4194320 | tf_op jit(solution)/shard_map/all_gather | solution.py:210
  417.1 17.2 %add_convert_fusion = bf16[2048,1024]{1,0:T(8,128)(2,1)} fusion(f32[2048,1024]{1,0:T(8,128)} %fusion.1, f32[2048,1024]{1,0:T(8,128)} %fusion.5, f32[2048,1024]{1,0:T(8,128)} %fusion.3, bf16[2048,1024]{1,0:T(8,128)(2,1)} %all-gather.14.cloned.1.call-done, bf16[4096,1024]{1,0:T(8,128)(2,1)} %all-gather.6.cloned.1.call-done), kind=kOutput, calls=%fused_computation | convolution fusion | flops 4303355904 | bytes 35651584 | tf_op jit(solution)/shard_map/dot_general | solution.py:211
  (52 shorter events, 15.5 us)
Async XLA Ops:
  6.5 75.8 %all-gather.6.cloned.1.call-start = ((), (), s32[]{:S(2)}) async-start(), calls=%async_computation.4 | async-start | bytes 9437184 | tf_op jit(solution)/shard_map/all_gather | solution.py:128
  25.8 2.2 copy-start
  28.0 2.2 copy-start.5
  30.2 30.7 %copy-start.14 = (f32[512,16]{0,1:T(8,128)S(1)}, f32[512,16]{0,1:T(8,128)}, u32[]{:S(2)}) copy-start(f32[512,16]{0,1:T(8,128)} %param.11) | copy-start | bytes 98308
  61.7 11.1 %all-to-all-start.2 = ((f32[4,16,512]{2,1,0:T(8,128)}), f32[4,16,512]{2,1,0:T(8,128)S(1)}, u32[]{:S(2)}, u32[]{:S(2)}) async-start(f32[4,16,512]{2,1,0:T(8,128)} %broadcast_in_dim.21), calls=%async_computation.2 | async-start | bytes 262144 | tf_op jit(solution)/shard_map/all_to_all | solution.py:118
  66.8 108.0 %all-gather.10.cloned.1.call-start = ((), (), s32[]{:S(2)}) async-start(), calls=%async_computation.6 | async-start | bytes 5242880 | tf_op jit(solution)/shard_map/all_gather | solution.py:210
  82.3 2.2 copy-start.1
  84.5 2.2 copy-start.6
  95.7 1.0 copy-start.10
  96.7 159.0 %all-gather.8.cloned.1.call-start = ((), (), s32[]{:S(2)}) async-start(), calls=%async_computation.5 | async-start | bytes 5242880 | tf_op jit(solution)/shard_map/all_gather | solution.py:210
  96.7 2.2 copy-start.2
  98.9 2.4 copy-start.7
  110.4 1.0 copy-start.11
  111.4 225.0 %all-gather.12.cloned.1.call-start = ((), (), s32[]{:S(2)}) async-start(), calls=%async_computation.7 | async-start | bytes 5242880 | tf_op jit(solution)/shard_map/all_gather | solution.py:210
  111.4 2.2 copy-start.3
  113.6 2.2 copy-start.8
  124.8 1.0 copy-start.12
  125.8 291.3 %all-gather.14.cloned.1.call-start = ((), (), s32[]{:S(2)}) async-start(), calls=%async_computation.8 | async-start | bytes 5242880 | tf_op jit(solution)/shard_map/all_gather | solution.py:210
  125.8 2.2 copy-start.4
  128.1 2.2 copy-start.9
  139.4 1.0 copy-start.13
Sparse Core Ops, SparseCore 0:
  9.2 60.6 all-gather.5
  96.8 77.9 all-gather.9
  176.3 79.2 all-gather.7
  257.1 79.2 all-gather.11
  337.8 79.2 all-gather.13

commit v2 on v1

--- a/solution.py
+++ b/solution.py
@@ -125,7 +125,12 @@
     chan_count = lax.axis_size("chan")
     length = float(tokens * chan_count * seq_count)
 
-    weight_rows = lax.all_gather(out_weight, "chan", axis=0, tiled=True)
+    def to_partner(block, distance):
+        pairs = [(s, s ^ distance) for s in range(seq_count)]
+        return lax.ppermute(block, "seq", pairs)
+
+    weight_own = lax.all_gather(out_weight, "chan", axis=0, tiled=True)
+    far_weight = to_partner(out_weight, 2)
 
     own_params = jnp.concatenate(
         [residue.T, pole_rate.T, skip_gain[None], jnp.zeros((7, own_channels), jnp.float32)], axis=0
@@ -135,7 +140,7 @@
     params = params.transpose(1, 0, 2).reshape(param_rows, channels)
 
     width = block_width(channels // PIECES)
-    limit = pltpu.CompilerParams(vmem_limit_bytes=40 * 1024 * 1024)
+    limit = pltpu.CompilerParams(vmem_limit_bytes=56 * 1024 * 1024)
     signal_scratch = pltpu.VMEM((tokens, LANES), jnp.float32)
 
     def columns(rows, base=0):
@@ -160,6 +165,8 @@
     )(params, key_rows, value_rows)
 
     finals = lax.all_to_all(final, "chan", split_axis=1, concat_axis=0, tiled=True)
+    finals, far_weight = lax.optimization_barrier((finals, far_weight))
+    weight_far = lax.all_gather(far_weight, "chan", axis=0, tiled=True)
     finals = finals.reshape(chan_count, order, own_channels)
     rates = pole_rate.T / length
     block_fade = jnp.exp(-rates * tokens)
@@ -179,10 +186,10 @@
     initial = lax.all_to_all(
         jnp.concatenate(entries, axis=0), "chan", split_axis=0, concat_axis=1, tiled=True
     )
-    initial, weight_rows = lax.optimization_barrier((initial, weight_rows))
+    initial, weight_own = lax.optimization_barrier((initial, weight_own))
 
     piece = channels // PIECES
-    result = jnp.zeros((seq_count * tokens, out_weight.shape[1]), jnp.float32)
+    near, partner = [], []
     for p in range(PIECES):
         base = p * piece // width
         spec = functools.partial(columns, base=base)
@@ -207,13 +214,29 @@
                 transcendentals=0,
             ),
         )(params, key_rows, value_rows, query_rows, ends, initial)
-        token_block = lax.all_gather(gated, "seq", axis=0, tiled=True)
-        result = result + jnp.dot(
-            token_block,
-            weight_rows[p * piece : (p + 1) * piece],
-            preferred_element_type=jnp.float32,
-        )
-    return result.astype(jnp.bfloat16).reshape(seq_count, tokens, out_weight.shape[1])
+        near.append(gated)
+        partner.append(to_partner(gated, 1))
+
+    def project(pieces, weight_rows):
+        terms = [
+            jnp.dot(
+                rows,
+                weight_rows[p * piece : (p + 1) * piece],
+                preferred_element_type=jnp.float32,
+            )
+            for p, rows in enumerate(pieces)
+        ]
+        return functools.reduce(jnp.add, terms).astype(jnp.bfloat16)
+
+    blocks = [None] * 4
+    blocks[2] = to_partner(project(near, weight_far), 2)
+    blocks[3] = to_partner(project(partner, weight_far), 2)
+    blocks[0] = project(near, weight_own)
+    blocks[1] = project(partner, weight_own)
+    result = jnp.zeros((seq_count, tokens, out_weight.shape[1]), jnp.bfloat16)
+    for distance, block in enumerate(blocks):
+        result = lax.dynamic_update_index_in_dim(result, block, own_range ^ distance, 0)
+    return result
 
 
 def solution(mesh):

time: 442 us -> 275 us (0.62)
  waiting for transfers between devices: 251 us -> 96.7 us
  local copies, waits for them, and re-layouts: 26.9 us -> 9.78 us
  starting transfers between devices: 5.27 us -> 15.9 us
  matrix products: 49.6 us -> 40.3 us
  blocking collectives: 39.3 us -> 31.2 us
  Pallas kernels: 54.3 us -> 59.8 us
  other arithmetic: 1.06 us -> 5.94 us
    all_gather x5 -> x2, waiting for transfers between devices: 244 us -> 0.01 us  [the longest x1 0.01 us: on_device(): weight_own = lax.all_gather(out_weight, 'chan', axis=0, tiled=True)]
    ppermute x0 -> x7, waiting for transfers between devices: none -> 80.1 us  [to_partner(): return lax.ppermute(block, 'seq', pairs)]
    unnamed x30 -> x20, local copies, waits for them, and re-layouts: 26 us -> 1.76 us
    all_to_all x0 -> x1, waiting for transfers between devices: none -> 9.98 us  [on_device(): lax.all_to_all(jnp.concatenate(entries, axis=0), 'chan', split_axis=0, co...]
    all_to_all x1 -> x0, blocking collectives: 9.35 us -> none  [on_device(): lax.all_to_all(jnp.concatenate(entries, axis=0), 'chan', split_axis=0, co...]
    dot_general x4 -> x16, matrix products: 49.6 us -> 40.3 us  [project(): jnp.dot(rows, weight_rows[p * piece:(p + 1) * piece], preferred_element_t...]
    ppermute x0 -> x7, starting transfers between devices: none -> 9.15 us  [to_partner(): return lax.ppermute(block, 'seq', pairs)]
  transfers between devices with their start and end apart: 6 -> 11, of which waited for: 5 -> 5; matrix products, arithmetic and copies ran while one was open for 8% -> 19% of each run, Pallas kernels for 10% -> 22%
where the time goes in v2:
time: 275 us; the launch traced here: 273 us
  waiting for transfers between devices  96.7 us (35%)
  Pallas kernels  59.8 us (22%)
  matrix products  40.3 us (15%)
  blocking collectives  31.2 us (11%)
  starting transfers between devices  15.9 us (6%)
  between operations  13.7 us (5%)
  local copies, waits for them, and re-layouts  9.78 us (4%)
  other arithmetic  5.94 us (2%)
    ppermute x7, waiting for transfers between devices, to_partner(): return lax.ppermute(block, 'seq', pairs)  80.1 us
    pallas_call x4, Pallas kernels, on_device(): pl.pallas_call(functools.partial(output_kernel, order, length), grid=(pie...  40.4 us
    dot_general x16, matrix products, project(): jnp.dot(rows, weight_rows[p * piece:(p + 1) * piece], preferred_element_t...  40.3 us
    pallas_call x1, Pallas kernels, on_device(): pl.pallas_call(functools.partial(state_kernel, order, length), grid=(chan...  19.4 us
    all_to_all x1, blocking collectives, copies_to_all(): return lax.all_to_all(copies, axis, split_axis=0, concat_axis=0, tiled=True)  18.7 us
    all_to_all x1, blocking collectives, on_device(): lax.all_to_all(final, 'chan', split_axis=1, concat_axis=0, tiled=True)  12.5 us
    all_to_all x1, waiting for transfers between devices, on_device(): lax.all_to_all(jnp.concatenate(entries, axis=0), 'chan', split_axis=0, co...  9.98 us
    ppermute x7, starting transfers between devices, to_partner(): return lax.ppermute(block, 'seq', pairs)  9.15 us
  transfers between devices with their start and end apart: 11, of which 5 were waited for; matrix products, arithmetic and copies ran while one was open for 19% of the time, Pallas kernels for 22%

profile of v2, /device:TPU:0, one launch (start us, length us, event | category | flops | bytes accessed | tf_op | source)
XLA Modules:
  0.0 273.3 jit_solution(12948859013638752195)
XLA Ops:
  7.3 4.1 %collective-permute-start = (bf16[512,1024]{1,0:T(8,128)(2,1)}, bf16[512,1024]{1,0:T(8,128)(2,1)S(1)}, u32[]{:S(2)}, u32[]{:S(2)}) collective-permute-start(bf16[512,1024]{1,0:T(8,128)(2,1)} %param.13), channel_id=1, source_target_pairs={{0,16},{8,24},{16,0},{24,8},{1,17},{9,25},{17,1},{25,9},{2,18},{10... | collective-permute-start | bytes 3145736 | tf_op jit(solution)/shard_map/ppermute | solution.py:130
  12.4 18.7 %all_to_all.48 = f32[8,40,512]{2,1,0:T(8,128)S(1)} all-to-all(f32[8,40,512]{2,1,0:T(8,128)S(1)} %broadcast_in_dim.37), channel_id=1, replica_groups=mesh['seq'=4,'chan'=8] {'chan'}, dimensions={0} | all-to-all | bytes 1310720 | tf_op jit(solution)/shard_map/all_to_all | solution.py:118
  32.1 19.4 %shard_map.73 = (f32[128,4096]{1,0:T(8,128)}, f32[16,4096]{1,0:T(8,128)}) custom-call(f32[40,4096]{1,0:T(8,128)} %bitcast.91, bf16[512,4096]{1,0:T(8,128)(2,1)} %key_ref.9, bf16[512,4096]{1,0:T(8,128)(2,1)} %value_ref.9), custom_call_target="tpu_custom_call" | custom-call | flops 67108864 | bytes 8388608 | tf_op jit(solution)/shard_map/pallas_call | solution.py:149
  52.5 12.5 %all_to_all.49 = f32[16,8,512]{2,0,1:T(8,128)S(1)} all-to-all(f32[16,8,512]{2,0,1:T(8,128)S(1)} %bitcast.113), channel_id=1, replica_groups=mesh['seq'=4,'chan'=8] {'chan'}, dimensions={1} | all-to-all | bytes 524288 | tf_op jit(solution)/shard_map/all_to_all | solution.py:167
  66.7 3.3 %all-to-all-start.2 = ((f32[4,16,512]{2,1,0:T(8,128)}), f32[4,16,512]{2,1,0:T(8,128)S(1)}, u32[]{:S(2)}, u32[]{:S(2)}) async-start(f32[4,16,512]{2,1,0:T(8,128)} %broadcast_in_dim.38), calls=%async_computation.2 | async-start | bytes 262144 | tf_op jit(solution)/shard_map/all_to_all | solution.py:118
  70.0 5.9 %all-to-all-done.2 = f32[4,16,512]{2,1,0:T(8,128)S(1)} async-done(((f32[4,16,512]{2,1,0:T(8,128)}), f32[4,16,512]{2,1,0:T(8,128)S(1)}, u32[]{:S(2)}, u32[]{:S(2)}) %all-to-all-start.2) | async-done | bytes 131104 | tf_op jit(solution)/shard_map/all_to_all | solution.py:118
  80.9 3.4 %all-to-all-start.3 = ((f32[8,16,512]{2,1,0:T(8,128)}), f32[8,16,512]{2,1,0:T(8,128)S(1)}, u32[]{:S(2)}, u32[]{:S(2)}) async-start(f32[8,16,512]{2,1,0:T(8,128)} %bitcast.9), calls=%async_computation.3 | async-start | bytes 524288 | tf_op jit(solution)/shard_map/all_to_all | solution.py:186
  84.4 10.0 %all-to-all-done.3 = f32[8,16,512]{2,1,0:T(8,128)S(1)} async-done(((f32[8,16,512]{2,1,0:T(8,128)}), f32[8,16,512]{2,1,0:T(8,128)S(1)}, u32[]{:S(2)}, u32[]{:S(2)}) %all-to-all-start.3) | async-done | bytes 262176 | tf_op jit(solution)/shard_map/all_to_all | solution.py:186
  95.1 10.1 %shard_map.77 = bf16[512,1024]{1,0:T(8,128)(2,1)} custom-call(f32[40,4096]{1,0:T(8,128)} %bitcast.92, bf16[512,4096]{1,0:T(8,128)(2,1)} %key_ref.9, bf16[512,4096]{1,0:T(8,128)(2,1)} %value_ref.9, bf16[512,4096]{1,0:T(8,128)(2,1)} %query_ref.7, f32[128,4096]{1,0:T(8,128)} %get-tuple-element.11.ends_ref, f32[16,4096]{1,0:T(8,128)} %bitcast.96), custom_call_target="tpu_custom_call" | custom-call | flops 33554432 | bytes 4194304 | tf_op jit(solution)/shard_map/pallas_call | solution.py:196
  106.4 10.1 %shard_map.76 = bf16[512,1024]{1,0:T(8,128)(2,1)} custom-call(f32[40,4096]{1,0:T(8,128)} %bitcast.93, bf16[512,4096]{1,0:T(8,128)(2,1)} %key_ref.9, bf16[512,4096]{1,0:T(8,128)(2,1)} %value_ref.9, bf16[512,4096]{1,0:T(8,128)(2,1)} %query_ref.7, f32[128,4096]{1,0:T(8,128)} %get-tuple-element.11.ends_ref, f32[16,4096]{1,0:T(8,128)} %bitcast.97), custom_call_target="tpu_custom_call" | custom-call | flops 33554432 | bytes 4194304 | tf_op jit(solution)/shard_map/pallas_call | solution.py:196
  117.2 10.1 %shard_map.74 = bf16[512,1024]{1,0:T(8,128)(2,1)} custom-call(f32[40,4096]{1,0:T(8,128)} %bitcast.94, bf16[512,4096]{1,0:T(8,128)(2,1)} %key_ref.9, bf16[512,4096]{1,0:T(8,128)(2,1)} %value_ref.9, bf16[512,4096]{1,0:T(8,128)(2,1)} %query_ref.7, f32[128,4096]{1,0:T(8,128)} %get-tuple-element.11.ends_ref, f32[16,4096]{1,0:T(8,128)} %bitcast.98), custom_call_target="tpu_custom_call" | custom-call | flops 33554432 | bytes 4194304 | tf_op jit(solution)/shard_map/pallas_call | solution.py:196
  128.7 10.1 %shard_map.75 = bf16[512,1024]{1,0:T(8,128)(2,1)} custom-call(f32[40,4096]{1,0:T(8,128)} %bitcast.95, bf16[512,4096]{1,0:T(8,128)(2,1)} %key_ref.9, bf16[512,4096]{1,0:T(8,128)(2,1)} %value_ref.9, bf16[512,4096]{1,0:T(8,128)(2,1)} %query_ref.7, f32[128,4096]{1,0:T(8,128)} %get-tuple-element.11.ends_ref, f32[16,4096]{1,0:T(8,128)} %bitcast.99), custom_call_target="tpu_custom_call" | custom-call | flops 33554432 | bytes 4194304 | tf_op jit(solution)/shard_map/pallas_call | solution.py:196
  139.6 2.8 %fusion.18 = f32[512,1024]{1,0:T(8,128)S(1)} fusion(bf16[512,1024]{1,0:T(8,128)(2,1)S(1)} %copy-done, bf16[4096,1024]{1,0:T(8,128)(2,1)} %all-gather.3.cloned.1.call-done), kind=kOutput, calls=%fused_computation.22 | convolution fusion | flops 1073741824 | bytes 5242880 | tf_op jit(solution)/shard_map/dot_general | solution.py:222
  142.5 2.9 %fusion.22 = f32[512,1024]{1,0:T(8,128)S(1)} fusion(bf16[512,1024]{1,0:T(8,128)(2,1)S(1)} %copy-done.4, bf16[4096,1024]{1,0:T(8,128)(2,1)} %all-gather.3.cloned.1.call-done), kind=kOutput, calls=%fused_computation.26 | convolution fusion | flops 1073741824 | bytes 5242880 | tf_op jit(solution)/shard_map/dot_general | solution.py:222
  145.4 2.9 %fusion.26 = f32[512,1024]{1,0:T(8,128)S(1)} fusion(bf16[512,1024]{1,0:T(8,128)(2,1)S(1)} %copy-done.5, bf16[4096,1024]{1,0:T(8,128)(2,1)} %all-gather.3.cloned.1.call-done), kind=kOutput, calls=%fused_computation.30 | convolution fusion | flops 1073741824 | bytes 5242880 | tf_op jit(solution)/shard_map/dot_general | solution.py:222
  148.3 2.5 broadcast_in_dim.34
  150.9 3.9 %fusion.37 = bf16[4,512,1024]{2,1,0:T(8,128)(2,1)} fusion(bf16[4,512,1024]{2,1,0:T(8,128)(2,1)} %broadcast_in_dim.34, s32[]{:T(128)S(6)} %select_n.39, f32[512,1024]{1,0:T(8,128)S(1)} %fusion.18, f32[512,1024]{1,0:T(8,128)S(1)} %fusion.22, f32[512,1024]{1,0:T(8,128)S(1)} %fusion.26, bf16[512,1024]{1,0:T(8,128)(2,1)S(1)} %copy-done.1, ...), kind=kOutput, calls=%fused_computation.37 | convolution fusion | flops 1075838976 | bytes 10485764 | tf_op jit(solution)/shard_map/dot_general | solution.py:222
  154.7 3.3 %fusion.6 = f32[512,1024]{1,0:T(8,128)S(1)} fusion(bf16[512,1024]{1,0:T(8,128)(2,1)} %shard_map.76, bf16[4096,1024]{1,0:T(8,128)(2,1)} %all-gather.5.cloned.1.call-done), kind=kOutput, calls=%fused_computation.10 | convolution fusion | flops 1073741824 | bytes 5242880 | tf_op jit(solution)/shard_map/dot_general | solution.py:222
  158.0 2.9 %fusion.14 = f32[512,1024]{1,0:T(8,128)S(1)} fusion(bf16[512,1024]{1,0:T(8,128)(2,1)S(1)} %copy-done.1, bf16[4096,1024]{1,0:T(8,128)(2,1)} %all-gather.5.cloned.1.call-done), kind=kOutput, calls=%fused_computation.18 | convolution fusion | flops 1073741824 | bytes 5242880 | tf_op jit(solution)/shard_map/dot_general | solution.py:222
  166.9 32.1 %collective-permute-done.1 = bf16[512,1024]{1,0:T(8,128)(2,1)} collective-permute-done((bf16[512,1024]{1,0:T(8,128)(2,1)}, bf16[512,1024]{1,0:T(8,128)(2,1)}, u32[]{:S(2)}, u32[]{:S(2)}) %collective-permute-start.1) | collective-permute-done | bytes 1048608 | tf_op jit(solution)/shard_map/ppermute | solution.py:130
  201.5 16.2 %collective-permute-done.2 = bf16[512,1024]{1,0:T(8,128)(2,1)} collective-permute-done((bf16[512,1024]{1,0:T(8,128)(2,1)}, bf16[512,1024]{1,0:T(8,128)(2,1)}, u32[]{:S(2)}, u32[]{:S(2)}) %collective-permute-start.2) | collective-permute-done | bytes 1048608 | tf_op jit(solution)/shard_map/ppermute | solution.py:130
  217.6 2.6 fusion.8
  222.5 2.7 fusion.20
  233.6 31.8 %collective-permute-done.6 = bf16[512,1024]{1,0:T(8,128)(2,1)S(1)} collective-permute-done((bf16[512,1024]{1,0:T(8,128)(2,1)S(1)}, bf16[512,1024]{1,0:T(8,128)(2,1)S(1)}, u32[]{:S(2)}, u32[]{:S(2)}) %collective-permute-start.6) | collective-permute-done | bytes 1048608 | tf_op jit(solution)/shard_map/ppermute | solution.py:130
  (64 shorter events, 35.2 us)
Async XLA Ops:
  6.5 88.5 %all-gather.3.cloned.1.call-start = ((), (), s32[]{:S(2)}) async-start(), calls=%async_computation.4 | async-start | bytes 9437184 | tf_op jit(solution)/shard_map/all_gather | solution.py:132
  7.3 147.5 %all-gather.5.cloned.1.call-start = ((), (), s32[]{:S(2)}) async-start(), calls=%async_computation.5 | async-start | bytes 9437184 | tf_op jit(solution)/shard_map/all_gather | solution.py:169
  7.3 57.6 %collective-permute-start = (bf16[512,1024]{1,0:T(8,128)(2,1)}, bf16[512,1024]{1,0:T(8,128)(2,1)S(1)}, u32[]{:S(2)}, u32[]{:S(2)}) collective-permute-start(bf16[512,1024]{1,0:T(8,128)(2,1)} %param.13), channel_id=1, source_target_pairs={{0,16},{8,24},{16,0},{24,8},{1,17},{9,25},{17,1},{25,9},{2,18},{10... | collective-permute-start | bytes 3145736 | tf_op jit(solution)/shard_map/ppermute | solution.py:130
  51.5 14.5 %copy-start.2 = (f32[512,16]{0,1:T(8,128)S(1)}, f32[512,16]{0,1:T(8,128)}, u32[]{:S(2)}) copy-start(f32[512,16]{0,1:T(8,128)} %param.11) | copy-start | bytes 98308
  64.9 1.0 copy-start.7
  66.7 9.2 %all-to-all-start.2 = ((f32[4,16,512]{2,1,0:T(8,128)}), f32[4,16,512]{2,1,0:T(8,128)S(1)}, u32[]{:S(2)}, u32[]{:S(2)}) async-start(f32[4,16,512]{2,1,0:T(8,128)} %broadcast_in_dim.38), calls=%async_computation.2 | async-start | bytes 262144 | tf_op jit(solution)/shard_map/all_to_all | solution.py:118
  80.9 13.4 %all-to-all-start.3 = ((f32[8,16,512]{2,1,0:T(8,128)}), f32[8,16,512]{2,1,0:T(8,128)S(1)}, u32[]{:S(2)}, u32[]{:S(2)}) async-start(f32[8,16,512]{2,1,0:T(8,128)} %bitcast.9), calls=%async_computation.3 | async-start | bytes 524288 | tf_op jit(solution)/shard_map/all_to_all | solution.py:186
  105.1 115.2 %collective-permute-start.4 = (bf16[512,1024]{1,0:T(8,128)(2,1)}, bf16[512,1024]{1,0:T(8,128)(2,1)S(1)}, u32[]{:S(2)}, u32[]{:S(2)}) collective-permute-start(bf16[512,1024]{1,0:T(8,128)(2,1)} %shard_map.77), channel_id=1, source_target_pairs={{0,8},{8,0},{16,24},{24,16},{1,9},{9,1},{17,25},{25,17},{2,10},{10... | collective-permute-start | bytes 3145736 | tf_op jit(solution)/shard_map/ppermute | solution.py:130
  116.5 47.9 %collective-permute-start.3 = (bf16[512,1024]{1,0:T(8,128)(2,1)}, bf16[512,1024]{1,0:T(8,128)(2,1)}, u32[]{:S(2)}, u32[]{:S(2)}) collective-permute-start(bf16[512,1024]{1,0:T(8,128)(2,1)} %shard_map.76), channel_id=1, source_target_pairs={{0,8},{8,0},{16,24},{24,16},{1,9},{9,1},{17,25},{25,17},{2,10},{10... | collective-permute-start | bytes 3145736 | tf_op jit(solution)/shard_map/ppermute | solution.py:130
  127.3 12.3 %copy-start = (bf16[512,1024]{1,0:T(8,128)(2,1)S(1)}, bf16[512,1024]{1,0:T(8,128)(2,1)}, u32[]{:S(2)}) copy-start(bf16[512,1024]{1,0:T(8,128)(2,1)} %shard_map.77) | copy-start | bytes 3145732
  127.3 71.6 %collective-permute-start.1 = (bf16[512,1024]{1,0:T(8,128)(2,1)}, bf16[512,1024]{1,0:T(8,128)(2,1)}, u32[]{:S(2)}, u32[]{:S(2)}) collective-permute-start(bf16[512,1024]{1,0:T(8,128)(2,1)} %shard_map.74), channel_id=1, source_target_pairs={{0,8},{8,0},{16,24},{24,16},{1,9},{9,1},{17,25},{25,17},{2,10},{10... | collective-permute-start | bytes 3145736 | tf_op jit(solution)/shard_map/ppermute | solution.py:130
  138.8 3.7 %copy-start.4 = (bf16[512,1024]{1,0:T(8,128)(2,1)S(1)}, bf16[512,1024]{1,0:T(8,128)(2,1)}, u32[]{:S(2)}) copy-start(bf16[512,1024]{1,0:T(8,128)(2,1)} %shard_map.76) | copy-start | bytes 3145732
  138.8 78.9 %collective-permute-start.2 = (bf16[512,1024]{1,0:T(8,128)(2,1)}, bf16[512,1024]{1,0:T(8,128)(2,1)}, u32[]{:S(2)}, u32[]{:S(2)}) collective-permute-start(bf16[512,1024]{1,0:T(8,128)(2,1)} %shard_map.75), channel_id=1, source_target_pairs={{0,8},{8,0},{16,24},{24,16},{1,9},{9,1},{17,25},{25,17},{2,10},{10... | collective-permute-start | bytes 3145736 | tf_op jit(solution)/shard_map/ppermute | solution.py:130
  142.5 3.0 %copy-start.5 = (bf16[512,1024]{1,0:T(8,128)(2,1)S(1)}, bf16[512,1024]{1,0:T(8,128)(2,1)}, u32[]{:S(2)}) copy-start(bf16[512,1024]{1,0:T(8,128)(2,1)} %shard_map.75) | copy-start | bytes 3145732
  148.3 2.6 copy-start.1
  154.7 6.3 %copy-start.3 = (bf16[4096,1024]{1,0:T(8,128)(2,1)S(1)}, bf16[4096,1024]{1,0:T(8,128)(2,1)}, u32[]{:S(2)}) copy-start(bf16[4096,1024]{1,0:T(8,128)(2,1)} %all-gather.5.cloned.1.call-done) | copy-start | bytes 25165828
  158.0 3.0 %copy-start.6 = (bf16[512,1024]{1,0:T(8,128)(2,1)S(1)}, bf16[512,1024]{1,0:T(8,128)(2,1)}, u32[]{:S(2)}) copy-start(bf16[512,1024]{1,0:T(8,128)(2,1)} %shard_map.75) | copy-start | bytes 3145732
  163.6 69.0 %collective-permute-start.5 = (bf16[512,1024]{1,0:T(8,128)(2,1)S(1)}, bf16[512,1024]{1,0:T(8,128)(2,1)S(1)}, u32[]{:S(2)}, u32[]{:S(2)}) collective-permute-start(bf16[512,1024]{1,0:T(8,128)(2,1)S(1)} %add_convert_fusion.1), channel_id=1, source_target_pairs={{0,16},{8,24},{16,0},{24,8},{1,17},{9,25},{17,1},{25,9},{2,18},{10... | collective-permute-start | bytes 3145736 | tf_op jit(solution)/shard_map/ppermute | solution.py:130
  217.6 4.1 %slice-start = ((s8[8388608]{0:T(1024)(128)(4,1)}), s8[4194304]{0:T(1024)(128)(4,1)S(1)}, s32[]{:S(2)}) async-start(s8[8388608]{0:T(1024)(128)(4,1)} %bitcast.110), calls=%async_computation.6 | async-start | bytes 8388608
  220.3 2.2 slice-start.1
  221.6 43.8 %collective-permute-start.6 = (bf16[512,1024]{1,0:T(8,128)(2,1)S(1)}, bf16[512,1024]{1,0:T(8,128)(2,1)S(1)}, u32[]{:S(2)}, u32[]{:S(2)}) collective-permute-start(bf16[512,1024]{1,0:T(8,128)(2,1)S(1)} %add_convert_fusion), channel_id=1, source_target_pairs={{0,16},{8,24},{16,0},{24,8},{1,17},{9,25},{17,1},{25,9},{2,18},{10... | collective-permute-start | bytes 3145736 | tf_op jit(solution)/shard_map/ppermute | solution.py:130
Sparse Core Ops, SparseCore 0:
  9.2 61.3 all-gather.2
  72.5 57.1 all-gather.4
